TPU v7x, 128 devices: a whole 4x4x4 slice. The times are simulated.
128 devices in a mesh: gx: 16 (over z, x), gy: 2 (over y_lo), gz: 4 (over y_hi, core).
Axes of the slice: x: 4, y: 4 (y_hi: 2, y_lo: 2; y = y_hi * 2 + y_lo), z: 4, core: 2. Of those that a mesh axis runs over, the one named last changes fastest.
Arguments:
- tensor: float32 [512, 768, 512], P('gx', 'gy', 'gz'), may hold values from -12 to 12
- factor_b: float32 [768, 64], P(('gy', 'gx', 'gz')), may hold values from -8 to 8
- factor_c: float32 [512, 64], P(('gz', 'gx', 'gy')), may hold values from -8 to 8
Outputs:
- factor_a_out: float32 [512, 64], P(('gx', 'gy', 'gz'))
- factor_b_out: float32 [768, 64], P(('gy', 'gx', 'gz'))
- factor_c_out: float32 [512, 64], P(('gz', 'gx', 'gy'))
All inputs are finite; a program needn't handle non-finite values.
Results may differ from a plain program's by a relative error of at most 0.0007.
Values sent between devices are 32-bit elements; how exact they have to be, the bound alone decides.
A program may use at most 64 MiB of HBM per device.

v0:
```python
import itertools

import jax
import jax.numpy as jnp
from jax import lax
from jax.experimental import pallas as pl
from jax.experimental.pallas import tpu as pltpu
from jax.sharding import PartitionSpec as P

MESH = pl.DeviceIdType.MESH
HIGHEST = lax.Precision.HIGHEST
F32 = jnp.float32
BF16 = jnp.bfloat16

RANK = 64
GROUP = 8
SIZES = {"z": 4, "x": 4, "yh": 2, "gy": 2, "core": 2}


def low(shape):
    return lax.broadcasted_iota(jnp.int32, shape, 1) < RANK


def swap(x):
    return pltpu.roll(x, RANK, 1)


def fold(x):
    return x + swap(x)


def compact(x):
    half = x.shape[0] // 2
    return jnp.where(low((half, 128)), x[:half], x[half:])


def expand(x):
    other = swap(x)
    side = low(x.shape)
    return jnp.concatenate([jnp.where(side, x, other), jnp.where(side, other, x)], axis=0)


def block_diagonal(x):
    side = low(x.shape)
    return jnp.concatenate([jnp.where(side, x, 0.0), jnp.where(side, 0.0, x)], axis=0)


def matmul(a, b):
    return jnp.dot(a, b, precision=HIGHEST, preferred_element_type=F32)


def gram_packed(x):
    full = matmul(x.T, x)
    own = jnp.where(low((RANK, 128)), full[:RANK] + swap(full[RANK:]), 0.0)
    return fold(own)


def scale_rows(gram, rows):
    r = lax.broadcasted_iota(jnp.int32, (RANK, 128), 0)
    c = lax.broadcasted_iota(jnp.int32, (RANK, 128), 1)
    both = jnp.where((c == r) | (c == r + RANK), gram, 0.0)
    across = jnp.sum(both, axis=0, keepdims=True)
    down = jnp.sum(jnp.where(c < RANK, both, 0.0), axis=1, keepdims=True)
    return jnp.sqrt(across / rows + 1e-06), jnp.sqrt(down / rows + 1e-06)


def inverse(system):
    lane = lax.broadcasted_iota(jnp.int32, (8, 128), 1) % RANK
    row = lax.broadcasted_iota(jnp.int32, (8, 128), 0)

    def row_of(x, n):
        return jnp.broadcast_to(x[n : n + 1], (8, 128))

    blocks = [system[8 * m : 8 * m + 8] for m in range(8)]
    for k in range(8):
        cols = [
            [jnp.broadcast_to(block[:, 8 * k + c : 8 * k + c + 1], (8, 128)) for c in range(8)]
            for block in blocks
        ]
        panel = (lane >= 8 * k) & (lane < 8 * k + 8)
        diag = list(cols[k])
        top = jnp.where(panel, jnp.where(lane == row + 8 * k, 1.0, 0.0), blocks[k])
        for c in range(8):
            pivot = 1.0 / row_of(diag[c], c)
            here = row == c
            factor = diag[c]
            line = row_of(top, c) * pivot
            top = jnp.where(here, line, top - factor * line)
            for d in range(c + 1, 8):
                line = row_of(diag[d], c) * pivot
                diag[d] = jnp.where(here, line, diag[d] - factor * line)
        lines = [row_of(top, c) for c in range(8)]
        for m in range(8):
            if m == k:
                blocks[m] = top
                continue
            less = [cols[m][c] * lines[c] for c in range(8)]
            while len(less) > 1:
                less = [less[n] + less[n + 1] for n in range(0, len(less), 2)]
            blocks[m] = jnp.where(panel, 0.0, blocks[m]) - less[0]
    return jnp.concatenate(blocks, axis=0)


def split(x):
    high = x.astype(BF16)
    return high, (x - high.astype(F32)).astype(BF16)


def kernel(
    t_ref, start_ref, out_ref,
    t32, thi, tlo, along, weights,
    c_one, c_all, b_one, b_all, b_packed,
    gb_slots, gc_slots, ma_part, ma_slots, ua_slots, ua_rows, a_columns,
    mb_part, mb_slots, mb_sum, ub, gu_slots, mc_part, mc_slot, mc_sum, ss_slots, rows_out,
    t_sem, send, recv, passed,
):
    gx, gy, gz = lax.axis_index("gx"), lax.axis_index("gy"), lax.axis_index("gz")
    z, x = gx // 4, lax.rem(gx, 4)
    yh, core = gz // 2, lax.rem(gz, 2)
    span_i = t_ref.shape[0]

    here = {"z": z, "x": x, "yh": yh, "gy": gy, "core": core}

    def group(*names):
        sizes = [SIZES[name] for name in names]

        def number(place):
            out = 0
            for name, size in zip(names, sizes):
                out = out * size + place[name]
            return out

        def hops(shift):
            shift = dict(zip(names, shift))
            y = 2 * shift.get("yh", 0) + shift.get("gy", 0)
            far = [min(n, 4 - n) for n in (shift.get("z", 0), shift.get("x", 0), y)]
            return sum(far) + 0.5 * shift.get("core", 0)

        shifts = sorted(itertools.product(*[range(size) for size in sizes]), key=hops, reverse=True)
        peers = []
        for shift in shifts[:-1]:
            place, source = dict(here), dict(here)
            for name, size, n in zip(names, sizes, shift):
                if n:
                    place[name] = lax.rem(here[name] + n, size)
                    source[name] = lax.rem(here[name] + size - n, size)
            device = (place["z"] * 4 + place["x"], place["gy"], place["yh"] * 2 + place["core"])
            peers.append((number(place), device, number(source)))
        return number(here), peers

    gy_me, gy_peers = group("gy")
    gz_me, gz_peers = group("yh", "core")
    gx_me, gx_peers = group("z", "x")
    _, x_peers = group("x")
    _, z_peers = group("z")
    yc_me, yc_peers = group("gy", "yh", "core")
    xc_me, xc_peers = group("x", "core")
    zh_me, zh_peers = group("z", "yh")

    pending = []
    used = [0]

    def start_one(peer, source, target):
        at = used[0]
        used[0] += 1
        copy = pltpu.make_async_remote_copy(
            src_ref=source,
            dst_ref=target,
            send_sem=send.at[at],
            recv_sem=recv.at[at],
            device_id=peer[1],
            device_id_type=MESH,
        )
        copy.start()
        pending.append(copy)
        return copy

    def start(peers, source, target):
        return [start_one(peer, source, target) for peer in peers]

    def arrive(copies):
        for copy in copies:
            copy.wait_recv()

    def add(total, copies, peers, slots):
        for copy, peer in zip(reversed(copies), reversed(peers)):
            copy.wait_recv()
            total = total + slots[peer[2]]
        return total

    def drain(keep=0):
        while len(pending) > keep:
            pending.pop(0).wait_send()

    barrier = pltpu.get_barrier_semaphore()
    greeted = z_peers + x_peers + yc_peers
    for peer in greeted:
        pl.semaphore_signal(barrier, inc=1, device_id=peer[1], device_id_type=MESH)
    c_one[gy] = start_ref[8:, :]
    b_one[gz] = start_ref[:8, :]

    def load(q):
        rows = pl.ds(q * GROUP, GROUP)
        return pltpu.make_async_copy(t_ref.at[rows], t32.at[rows], t_sem.at[q])

    def split_tensor(q, _):
        load(q).wait()

        def one(i, _):
            thi[i], tlo[i] = split(t32[i])
            return 0

        lax.fori_loop(q * GROUP, (q + 1) * GROUP, one, 0)
        return 0

    pl.semaphore_wait(barrier, len(greeted))

    for peer in z_peers:
        pl.semaphore_signal(passed, inc=1, device_id=peer[1], device_id_type=MESH)
    c_first = start(gy_peers, start_ref.at[pl.ds(8, 8)], c_one.at[gy])
    b_first = start(gz_peers, start_ref.at[pl.ds(0, 8)], b_one.at[gz])
    for q in range(span_i // GROUP):
        load(q).start()
    arrive(c_first)
    c_all[gx] = jnp.concatenate([c_one[0][:4], c_one[1][:4]], axis=1)
    pl.semaphore_wait(passed, len(z_peers))
    c_second = start(gx_peers, c_all.at[gx], c_all.at[gx])
    arrive(b_first)
    b_all[gx] = jnp.concatenate(
        [
            jnp.concatenate([b_one[0][:6], b_one[2][:6]], axis=1),
            jnp.concatenate([b_one[1][:6], b_one[3][:6]], axis=1),
        ],
        axis=0,
    )
    b_second = start(gx_peers, b_all.at[gx], b_all.at[gx])
    lax.fori_loop(0, span_i // GROUP, split_tensor, 0)
    drain(30)
    arrive(c_second)
    pieces = []
    for g in range(16):
        piece = c_all[g]
        other = swap(piece)
        side = low((4, 128))
        pieces += [jnp.where(side, piece, other), jnp.where(side, other, piece)]
    block_c = jnp.concatenate(pieces, axis=0)
    gram_c = matmul(block_c.T, block_c)[:RANK]
    gc_slots[gz] = compact(gram_c)
    gc_copies = start(gz_peers, gc_slots.at[gz], gc_slots.at[gz])
    c_high, c_low = split(block_c)
    side = low((128, 128))
    none = jnp.zeros((128, 128), BF16)
    weights[:128, :128] = jnp.where(side, c_high, none)
    weights[:128, 128:] = jnp.where(side, c_low, none)
    weights[128:, :128] = jnp.where(side, none, c_high)
    weights[128:, 128:] = jnp.where(side, none, c_low)

    half_j = along.shape[1]

    def wide(ref):
        return jnp.concatenate([ref[:, :half_j, :], ref[:, half_j:, :]], axis=2).reshape(span_i * half_j, 256)

    both = jnp.dot(wide(thi), weights[...], preferred_element_type=F32)
    rest = jnp.dot(wide(tlo), weights[:, :128], preferred_element_type=F32)
    along[...] = (both[:, :128] + (both[:, 128:] + rest)).reshape(along.shape)
    arrive(b_second)
    for g in range(8):
        one, two = b_all[g], b_all[g + 8]
        side = low((12, 128))
        b_packed[24 * g : 24 * g + 12, :] = jnp.where(side, one, swap(two))
        b_packed[24 * g + 12 : 24 * g + 24, :] = jnp.where(side, swap(one), two)
    block_b = b_packed[...]
    gb_slots[gy] = compact(gram_packed(block_b))
    gb_copies = start(gy_peers, gb_slots.at[gy], gb_slots.at[gy])
    def moment_a(i, _):
        product = along[i] * block_b
        ma_part[i] = jnp.sum(product.reshape(half_j // 8, 8, 128), axis=0)
        return 0

    lax.fori_loop(0, span_i, moment_a, 0)
    ma_slots[yc_me] = compact(fold(jnp.sum(ma_part[...], axis=1)))
    ma_copies = start(yc_peers, ma_slots.at[yc_me], ma_slots.at[yc_me])
    drain(7)
    arrive(gc_copies)
    arrive(gb_copies)
    gram_c = expand(gc_slots[0] + gc_slots[1] + gc_slots[2] + gc_slots[3])
    gram_b = expand(gb_slots[0] + gb_slots[1])
    inverse_a = block_diagonal(inverse(gram_b * gram_c))
    ua = matmul(add(ma_slots[yc_me], ma_copies, yc_peers, ma_slots), inverse_a)
    ua_slots[gx] = ua
    rows_a = expand(ua)
    for i in range(32):
        ua_rows[i] = jnp.broadcast_to(rows_a[i : i + 1], (8, 128))

    def moment_b(chunk):
        rows = pl.ds(pl.multiple_of(chunk * 24, 8), 24)
        total = jnp.zeros((3, 8, 128), F32)
        for q in range(4):
            some = along[8 * q : 8 * q + 8, rows, :].reshape(8, 3, 8, 128)
            total = total + jnp.sum(some * ua_rows[8 * q : 8 * q + 8][:, None], axis=0)
        return total.reshape(24, 128)

    mb_copies = []
    for peer in xc_peers:
        mb_part[peer[0]] = moment_b(peer[0])
        mb_copies.append(start_one(peer, mb_part.at[peer[0]], mb_slots.at[xc_me]))
    ua_copies = start(gx_peers, ua_slots.at[gx], ua_slots.at[gx])
    moment = moment_b(xc_me)
    drain(22)
    mb_sum[zh_me] = add(moment, mb_copies, xc_peers, mb_slots)
    mb_copies = start(zh_peers, mb_sum.at[zh_me], mb_sum.at[zh_me])
    arrive(ua_copies)
    gram_ua = gram_packed(ua_slots[...].reshape(256, 128))
    scale_a, scale_a_down = scale_rows(gram_ua, float(span_i * 16))
    gram_a = gram_ua / (scale_a * scale_a_down)
    inverse_b = block_diagonal(inverse(gram_a * gram_c))
    unscale_a = 1.0 / scale_a
    shard_a = ua_slots[gx] / scale_a
    full_a = expand(shard_a)
    turned = jnp.concatenate([full_a, full_a, full_a, full_a], axis=0).T
    for i in range(32):
        a_columns[i] = jnp.broadcast_to(turned[:RANK, i : i + 1], (RANK, 128))
    rows_out[:16, :] = jnp.where(gy == 0, shard_a, swap(shard_a))
    out_ref[:4, :] = rows_out[pl.ds(gz * 4, 4), :]
    drain(7)
    moment = add(mb_sum[zh_me], mb_copies, zh_peers, mb_sum)
    ub[xc_me] = matmul(moment * unscale_a, inverse_b)
    ub_copies = start(xc_peers, ub.at[xc_me], ub.at[xc_me])
    drain(7)
    arrive(ub_copies)

    block_b = ub[...].reshape(half_j, 128)
    turned = block_b.T
    turned_high, turned_low = split(turned)
    left = [
        jnp.concatenate([turned_high[h * RANK : (h + 1) * RANK], turned_low[h * RANK : (h + 1) * RANK]], axis=0)
        for h in range(2)
    ]
    left = jnp.concatenate(left, axis=1)

    moment = jnp.zeros((RANK, 128), F32)
    for i in range(0, span_i, 2):
        high = jnp.concatenate([thi[i], thi[i + 1]], axis=1)
        rest = jnp.concatenate([tlo[i], tlo[i + 1]], axis=1)
        part = jnp.dot(left, high, preferred_element_type=F32)
        part = part[:RANK] + (part[RANK:] + jnp.dot(left[:RANK], rest, preferred_element_type=F32))
        moment = moment + (part[:, :128] * a_columns[i] + part[:, 128:] * a_columns[i + 1])
    moment = compact(jnp.concatenate([moment, moment], axis=0).T)
    upper = lax.broadcasted_iota(jnp.int32, (8, 128), 0) < 4
    parts = [[], []]
    for m in range(4):
        one, two = moment[16 * m : 16 * m + 8], moment[16 * m + 8 : 16 * m + 16]
        parts[0].append(jnp.where(upper, one, pltpu.roll(two, 4, 0)))
        parts[1].append(jnp.where(upper, pltpu.roll(one, 4, 0), two))
    parts = [jnp.concatenate(part, axis=0) for part in parts]
    mc_part[...] = jnp.where(gy == 0, parts[1], parts[0])
    mc_copies = start(gy_peers, mc_part, mc_slot)
    gu_slots[gy] = compact(gram_packed(block_b))
    gu_copies = start(gy_peers, gu_slots.at[gy], gu_slots.at[gy])
    drain(2)
    arrive(mc_copies)
    mc_sum[gx] = jnp.where(gy == 0, parts[0], parts[1]) + mc_slot[...]
    mc_copies = start(gx_peers, mc_sum.at[gx], mc_sum.at[gx])
    arrive(gu_copies)
    gram_ub = expand(gu_slots[0] + gu_slots[1])
    scale_b, scale_b_down = scale_rows(gram_ub, float(half_j * 4))
    gram_b = gram_ub / (scale_b * scale_b_down)
    inverse_c = block_diagonal(inverse(gram_a * gram_b))
    unscale_b = 1.0 / scale_b
    shard_b = block_b / scale_b
    b_packed[...] = jnp.where(z // 2 == 0, shard_b, swap(shard_b))
    first = lax.rem(z, 2) * 96 + x * 24 + yh * 12 + core * 6
    out_ref[8:14, :] = b_packed[pl.ds(first, 6), :]
    drain(15)
    moment = add(mc_sum[gx], mc_copies, gx_peers, mc_sum)
    uc = matmul(moment * unscale_b, inverse_c)
    ss_slots[yc_me] = fold(jnp.sum(uc * uc, axis=0, keepdims=True))
    ss_copies = start(yc_peers, ss_slots.at[yc_me], ss_slots.at[yc_me])
    rows_out[...] = jnp.where(z // 2 == 0, uc, swap(uc))
    own = rows_out[pl.ds(lax.rem(gx, 8) * 4, 4), :]
    drain(7)
    total = add(ss_slots[yc_me], ss_copies, yc_peers, ss_slots)
    out_ref[4:8, :] = own / jnp.sqrt(total / float(128 * 4) + 1e-06)
    drain()


COPIES = 1 + 3 + 15 + 15 + 3 + 1 + 7 + 7 + 15 + 7 + 7 + 1 + 1 + 15 + 7


def local(tensor, factor_b, factor_c):
    span_i, span_j, span_k = tensor.shape
    half_j = span_j // 2
    vmem = pl.BlockSpec(memory_space=pltpu.VMEM)
    scratch = [
        pltpu.VMEM(tensor.shape, F32),
        pltpu.VMEM(tensor.shape, BF16),
        pltpu.VMEM(tensor.shape, BF16),
        pltpu.VMEM((span_i, half_j, 128), F32),
        pltpu.VMEM((256, 256), BF16),
        pltpu.VMEM((2, 8, RANK), F32),
        pltpu.VMEM((16, 4, 128), F32),
        pltpu.VMEM((4, 8, RANK), F32),
        pltpu.VMEM((16, 12, 128), F32),
        pltpu.VMEM((half_j, 128), F32),
        pltpu.VMEM((2, 32, 128), F32),
        pltpu.VMEM((4, 32, 128), F32),
        pltpu.VMEM((span_i, 8, 128), F32),
        pltpu.VMEM((8, 16, 128), F32),
        pltpu.VMEM((16, 16, 128), F32),
        pltpu.VMEM((32, 8, 128), F32),
        pltpu.VMEM((32, RANK, 128), F32),
        pltpu.VMEM((8, 24, 128), F32),
        pltpu.VMEM((8, 24, 128), F32),
        pltpu.VMEM((8, 24, 128), F32),
        pltpu.VMEM((8, 24, 128), F32),
        pltpu.VMEM((2, 32, 128), F32),
        pltpu.VMEM((32, 128), F32),
        pltpu.VMEM((32, 128), F32),
        pltpu.VMEM((16, 32, 128), F32),
        pltpu.VMEM((8, 1, 128), F32),
        pltpu.VMEM((32, 128), F32),
        pltpu.SemaphoreType.DMA((span_i // GROUP,)),
        pltpu.SemaphoreType.DMA((COPIES,)),
        pltpu.SemaphoreType.DMA((COPIES,)),
        pltpu.SemaphoreType.REGULAR,
    ]
    start = jnp.concatenate(
        [jnp.pad(factor_b, ((0, 2), (0, 0))), jnp.pad(factor_c, ((0, 4), (0, 0)))], axis=0
    )
    out = pl.pallas_call(
        kernel,
        out_shape=jax.ShapeDtypeStruct((16, 128), F32),
        in_specs=[pl.BlockSpec(memory_space=pl.ANY), vmem],
        out_specs=vmem,
        scratch_shapes=scratch,
        compiler_params=pltpu.CompilerParams(
            collective_id=0, has_side_effects=True, vmem_limit_bytes=48 * 1024 * 1024
        ),
    )(tensor, start)
    return out[:4, :RANK], out[8:14, :RANK], out[4:8, :RANK]


def solution(mesh):
    return jax.shard_map(
        local,
        mesh=mesh,
        in_specs=(P("gx", "gy", "gz"), P(("gy", "gx", "gz"), None), P(("gz", "gx", "gy"), None)),
        out_specs=(
            P(("gx", "gy", "gz"), None),
            P(("gy", "gx", "gz"), None),
            P(("gz", "gx", "gy"), None),
        ),
        check_vma=False,
    )
```

profile of v0, /device:TPU:1, one launch (start us, length us, event | category | flops | bytes accessed | tf_op | source)
XLA Modules:
  0.0 53.3 jit_solution(7370162795253588506)
XLA Ops:
  0.6 0.7 %select_maximum_fusion.start_ref = f32[16,64]{1,0:T(8,128)S(1)} fusion(f32[4,64]{1,0:T(4,128)} %param.5, f32[6,64]{1,0:T(8,128)} %param.4), kind=kLoop, calls=%fused_computation | loop fusion | flops 5120 | bytes 6656 | tf_op jit(solution)/shard_map/concatenate | solution.py:427
  1.3 50.7 %shard_map.58 = f32[16,128]{1,0:T(8,128)S(1)} custom-call(f32[32,384,128]{2,1,0:T(8,128)} %t_ref.1, f32[16,64]{1,0:T(8,128)S(1)} %select_maximum_fusion.start_ref), custom_call_target="tpu_custom_call" | custom-call | tf_op jit(solution)/shard_map/pallas_call | solution.py:430
  52.1 0.6 %fusion = (f32[4,64]{1,0:T(4,128)}, f32[4,64]{1,0:T(4,128)}) fusion(f32[16,128]{1,0:T(8,128)S(1)} %shard_map.58), kind=kLoop, calls=%fused_computation.3 | loop fusion | bytes 4096 | tf_op jit(solution)/shard_map/slice | solution.py:440
  52.7 0.6 %slice.10 = f32[6,64]{1,0:T(8,128)} slice(f32[16,128]{1,0:T(8,128)S(1)} %shard_map.58), slice={[8:14], [0:64]} | slice | bytes 3072 | tf_op jit(solution)/shard_map/slice | solution.py:440
where the time goes:
time: 53.4 us; the launch traced here: 53.3 us
  Pallas kernels  50.7 us (95%)
  local copies, waits for them, and re-layouts  1.18 us (2%)
  other arithmetic  0.71 us (1%)
  between operations  0.64 us (1%)
    pallas_call x1, Pallas kernels, local(): pl.pallas_call(kernel, out_shape=jax.ShapeDtypeStruct((16, 128), F32), in...  50.7 us
    slice x2, local copies, waits for them, and re-layouts, local(): return (out[:4, :RANK], out[8:14, :RANK], out[4:8, :RANK])  1.18 us

commit v1 on v0

--- a/solution.py
+++ b/solution.py
@@ -146,16 +146,16 @@
                     source[name] = lax.rem(here[name] + size - n, size)
             device = (place["z"] * 4 + place["x"], place["gy"], place["yh"] * 2 + place["core"])
             peers.append((number(place), device, number(source)))
-        return number(here), peers
-
-    gy_me, gy_peers = group("gy")
-    gz_me, gz_peers = group("yh", "core")
-    gx_me, gx_peers = group("z", "x")
-    _, x_peers = group("x")
-    _, z_peers = group("z")
-    yc_me, yc_peers = group("gy", "yh", "core")
-    xc_me, xc_peers = group("x", "core")
-    zh_me, zh_peers = group("z", "yh")
+        return number(here), peers, shifts[:-1]
+
+    gy_me, gy_peers, _ = group("gy")
+    gz_me, gz_peers, _ = group("yh", "core")
+    gx_me, gx_peers, _ = group("z", "x")
+    _, x_peers, _ = group("x")
+    _, z_peers, _ = group("z")
+    yc_me, yc_peers, _ = group("gy", "yh", "core")
+    xc_me, xc_peers, xc_shifts = group("x", "core")
+    zh_me, zh_peers, _ = group("z", "yh")
 
     pending = []
     used = [0]
@@ -222,7 +222,8 @@
     for q in range(span_i // GROUP):
         load(q).start()
     arrive(c_first)
-    c_all[gx] = jnp.concatenate([c_one[0][:4], c_one[1][:4]], axis=1)
+    rows_c = jnp.concatenate([c_one[0][:4], c_one[1][:4]], axis=0)
+    c_all[gx] = jnp.concatenate([rows_c, rows_c], axis=1)
     pl.semaphore_wait(passed, len(z_peers))
     c_second = start(gx_peers, c_all.at[gx], c_all.at[gx])
     arrive(b_first)
@@ -237,13 +238,7 @@
     lax.fori_loop(0, span_i // GROUP, split_tensor, 0)
     drain(30)
     arrive(c_second)
-    pieces = []
-    for g in range(16):
-        piece = c_all[g]
-        other = swap(piece)
-        side = low((4, 128))
-        pieces += [jnp.where(side, piece, other), jnp.where(side, other, piece)]
-    block_c = jnp.concatenate(pieces, axis=0)
+    block_c = c_all[...].reshape(128, 128)
     gram_c = matmul(block_c.T, block_c)[:RANK]
     gc_slots[gz] = compact(gram_c)
     gc_copies = start(gz_peers, gc_slots.at[gz], gc_slots.at[gz])
@@ -257,12 +252,6 @@
 
     half_j = along.shape[1]
 
-    def wide(ref):
-        return jnp.concatenate([ref[:, :half_j, :], ref[:, half_j:, :]], axis=2).reshape(span_i * half_j, 256)
-
-    both = jnp.dot(wide(thi), weights[...], preferred_element_type=F32)
-    rest = jnp.dot(wide(tlo), weights[:, :128], preferred_element_type=F32)
-    along[...] = (both[:, :128] + (both[:, 128:] + rest)).reshape(along.shape)
     arrive(b_second)
     for g in range(8):
         one, two = b_all[g], b_all[g + 8]
@@ -272,12 +261,18 @@
     block_b = b_packed[...]
     gb_slots[gy] = compact(gram_packed(block_b))
     gb_copies = start(gy_peers, gb_slots.at[gy], gb_slots.at[gy])
-    def moment_a(i, _):
-        product = along[i] * block_b
-        ma_part[i] = jnp.sum(product.reshape(half_j // 8, 8, 128), axis=0)
-        return 0
-
-    lax.fori_loop(0, span_i, moment_a, 0)
+    for q in range(0, span_i, 2):
+
+        def wide(ref):
+            left, right = ref[q : q + 2, :half_j, :], ref[q : q + 2, half_j:, :]
+            return jnp.concatenate([left, right], axis=2).reshape(2 * half_j, 256)
+
+        both = jnp.dot(wide(thi), weights[...], preferred_element_type=F32)
+        rest = jnp.dot(wide(tlo), weights[:, :128], preferred_element_type=F32)
+        pair = (both[:, :128] + (both[:, 128:] + rest)).reshape(2, half_j, 128)
+        along[q : q + 2] = pair
+        for n in range(2):
+            ma_part[q + n] = jnp.sum((pair[n] * block_b).reshape(half_j // 8, 8, 128), axis=0)
     ma_slots[yc_me] = compact(fold(jnp.sum(ma_part[...], axis=1)))
     ma_copies = start(yc_peers, ma_slots.at[yc_me], ma_slots.at[yc_me])
     drain(7)
@@ -315,6 +310,9 @@
     gram_a = gram_ua / (scale_a * scale_a_down)
     inverse_b = block_diagonal(inverse(gram_a * gram_c))
     unscale_a = 1.0 / scale_a
+    moment = add(mb_sum[zh_me], mb_copies, zh_peers, mb_sum)
+    ub[xc_me] = matmul(moment * unscale_a, inverse_b)
+    ub_copies = start(xc_peers, ub.at[xc_me], ub.at[xc_me])
     shard_a = ua_slots[gx] / scale_a
     full_a = expand(shard_a)
     turned = jnp.concatenate([full_a, full_a, full_a, full_a], axis=0).T
@@ -323,28 +321,40 @@
     rows_out[:16, :] = jnp.where(gy == 0, shard_a, swap(shard_a))
     out_ref[:4, :] = rows_out[pl.ds(gz * 4, 4), :]
     drain(7)
-    moment = add(mb_sum[zh_me], mb_copies, zh_peers, mb_sum)
-    ub[xc_me] = matmul(moment * unscale_a, inverse_b)
-    ub_copies = start(xc_peers, ub.at[xc_me], ub.at[xc_me])
-    drain(7)
-    arrive(ub_copies)
-
+    arrivals = list(zip(ub_copies, xc_peers, xc_shifts))
+    moment = jnp.zeros((RANK, 128), F32)
+    for near in (True, False):
+        for copy, peer, shift in reversed(arrivals):
+            if (shift[0] in (0, 1)) == near:
+                copy.wait_recv()
+        ends = [x, lax.rem(x + 3, 4)] if near else [lax.rem(x + 1, 4), lax.rem(x + 2, 4)]
+        own = [ub[pl.ds(2 * end, 2)].reshape(48, 128) for end in ends]
+        turned_high, turned_low = split(jnp.concatenate(own, axis=0).T)
+        left = jnp.concatenate(
+            [
+                jnp.concatenate([turned_high[:RANK], turned_high[RANK:]], axis=1),
+                jnp.concatenate([turned_low[:RANK], turned_low[RANK:]], axis=1),
+            ],
+            axis=0,
+        )
+
+        def rows_of(ref, i):
+            return jnp.concatenate(
+                [
+                    ref[i, pl.ds(pl.multiple_of(h * half_j + end * 48, 16), 48), :]
+                    for h in range(2)
+                    for end in ends
+                ],
+                axis=0,
+            )
+
+        for i in range(0, span_i, 2):
+            high = jnp.concatenate([rows_of(thi, i), rows_of(thi, i + 1)], axis=1)
+            rest = jnp.concatenate([rows_of(tlo, i), rows_of(tlo, i + 1)], axis=1)
+            part = jnp.dot(left, high, preferred_element_type=F32)
+            part = part[:RANK] + (part[RANK:] + jnp.dot(left[:RANK], rest, preferred_element_type=F32))
+            moment = moment + (part[:, :128] * a_columns[i] + part[:, 128:] * a_columns[i + 1])
     block_b = ub[...].reshape(half_j, 128)
-    turned = block_b.T
-    turned_high, turned_low = split(turned)
-    left = [
-        jnp.concatenate([turned_high[h * RANK : (h + 1) * RANK], turned_low[h * RANK : (h + 1) * RANK]], axis=0)
-        for h in range(2)
-    ]
-    left = jnp.concatenate(left, axis=1)
-
-    moment = jnp.zeros((RANK, 128), F32)
-    for i in range(0, span_i, 2):
-        high = jnp.concatenate([thi[i], thi[i + 1]], axis=1)
-        rest = jnp.concatenate([tlo[i], tlo[i + 1]], axis=1)
-        part = jnp.dot(left, high, preferred_element_type=F32)
-        part = part[:RANK] + (part[RANK:] + jnp.dot(left[:RANK], rest, preferred_element_type=F32))
-        moment = moment + (part[:, :128] * a_columns[i] + part[:, 128:] * a_columns[i + 1])
     moment = compact(jnp.concatenate([moment, moment], axis=0).T)
     upper = lax.broadcasted_iota(jnp.int32, (8, 128), 0) < 4
     parts = [[], []]
@@ -398,7 +408,7 @@
         pltpu.VMEM((span_i, half_j, 128), F32),
         pltpu.VMEM((256, 256), BF16),
         pltpu.VMEM((2, 8, RANK), F32),
-        pltpu.VMEM((16, 4, 128), F32),
+        pltpu.VMEM((16, 8, 128), F32),
         pltpu.VMEM((4, 8, RANK), F32),
         pltpu.VMEM((16, 12, 128), F32),
         pltpu.VMEM((half_j, 128), F32),

time: 53.4 us -> 52.7 us (0.987)
  Pallas kernels: 50.7 us -> 50 us
    pallas_call x1, Pallas kernels: 50.7 us -> 50 us  [local(): pl.pallas_call(kernel, out_shape=jax.ShapeDtypeStruct((16, 128), F32), in...]
where the time goes in v1:
time: 52.7 us; the launch traced here: 52.6 us
  Pallas kernels  50 us (95%)
  local copies, waits for them, and re-layouts  1.18 us (2%)
  other arithmetic  0.71 us (1%)
  between operations  0.64 us (1%)
    pallas_call x1, Pallas kernels, local(): pl.pallas_call(kernel, out_shape=jax.ShapeDtypeStruct((16, 128), F32), in...  50 us
    slice x2, local copies, waits for them, and re-layouts, local(): return (out[:4, :RANK], out[8:14, :RANK], out[4:8, :RANK])  1.18 us

profile of v1, /device:TPU:1, one launch (start us, length us, event | category | flops | bytes accessed | tf_op | source)
XLA Modules:
  0.0 52.6 jit_solution(14346000373927187702)
XLA Ops:
  0.6 0.7 %select_maximum_fusion.start_ref = f32[16,64]{1,0:T(8,128)S(1)} fusion(f32[4,64]{1,0:T(4,128)} %param.5, f32[6,64]{1,0:T(8,128)} %param.4), kind=kLoop, calls=%fused_computation | loop fusion | flops 5120 | bytes 6656 | tf_op jit(solution)/shard_map/concatenate | solution.py:437
  1.3 50.0 %shard_map.58 = f32[16,128]{1,0:T(8,128)S(1)} custom-call(f32[32,384,128]{2,1,0:T(8,128)} %t_ref.1, f32[16,64]{1,0:T(8,128)S(1)} %select_maximum_fusion.start_ref), custom_call_target="tpu_custom_call" | custom-call | tf_op jit(solution)/shard_map/pallas_call | solution.py:440
  51.4 0.6 %fusion = (f32[4,64]{1,0:T(4,128)}, f32[4,64]{1,0:T(4,128)}) fusion(f32[16,128]{1,0:T(8,128)S(1)} %shard_map.58), kind=kLoop, calls=%fused_computation.3 | loop fusion | bytes 4096 | tf_op jit(solution)/shard_map/slice | solution.py:450
  52.0 0.6 %slice.10 = f32[6,64]{1,0:T(8,128)} slice(f32[16,128]{1,0:T(8,128)S(1)} %shard_map.58), slice={[8:14], [0:64]} | slice | bytes 3072 | tf_op jit(solution)/shard_map/slice | solution.py:450

commit v2 on v1

--- a/solution.py
+++ b/solution.py
@@ -258,7 +258,7 @@
         side = low((12, 128))
         b_packed[24 * g : 24 * g + 12, :] = jnp.where(side, one, swap(two))
         b_packed[24 * g + 12 : 24 * g + 24, :] = jnp.where(side, swap(one), two)
-    block_b = b_packed[...]
+    block_b = b_packed[:half_j, :]
     gb_slots[gy] = compact(gram_packed(block_b))
     gb_copies = start(gy_peers, gb_slots.at[gy], gb_slots.at[gy])
     for q in range(0, span_i, 2):
@@ -378,7 +378,7 @@
     inverse_c = block_diagonal(inverse(gram_a * gram_b))
     unscale_b = 1.0 / scale_b
     shard_b = block_b / scale_b
-    b_packed[...] = jnp.where(z // 2 == 0, shard_b, swap(shard_b))
+    b_packed[:half_j, :] = jnp.where(z // 2 == 0, shard_b, swap(shard_b))
     first = lax.rem(z, 2) * 96 + x * 24 + yh * 12 + core * 6
     out_ref[8:14, :] = b_packed[pl.ds(first, 6), :]
     drain(15)
@@ -386,7 +386,7 @@
     uc = matmul(moment * unscale_b, inverse_c)
     ss_slots[yc_me] = fold(jnp.sum(uc * uc, axis=0, keepdims=True))
     ss_copies = start(yc_peers, ss_slots.at[yc_me], ss_slots.at[yc_me])
-    rows_out[...] = jnp.where(z // 2 == 0, uc, swap(uc))
+    rows_out[:32, :] = jnp.where(z // 2 == 0, uc, swap(uc))
     own = rows_out[pl.ds(lax.rem(gx, 8) * 4, 4), :]
     drain(7)
     total = add(ss_slots[yc_me], ss_copies, yc_peers, ss_slots)
@@ -410,8 +410,8 @@
         pltpu.VMEM((2, 8, RANK), F32),
         pltpu.VMEM((16, 8, 128), F32),
         pltpu.VMEM((4, 8, RANK), F32),
-        pltpu.VMEM((16, 12, 128), F32),
-        pltpu.VMEM((half_j, 128), F32),
+        pltpu.VMEM((17, 12, 128), F32),
+        pltpu.VMEM((half_j + 8, 128), F32),
         pltpu.VMEM((2, 32, 128), F32),
         pltpu.VMEM((4, 32, 128), F32),
         pltpu.VMEM((span_i, 8, 128), F32),
@@ -427,8 +427,8 @@
         pltpu.VMEM((32, 128), F32),
         pltpu.VMEM((32, 128), F32),
         pltpu.VMEM((16, 32, 128), F32),
-        pltpu.VMEM((8, 1, 128), F32),
-        pltpu.VMEM((32, 128), F32),
+        pltpu.VMEM((16, 1, 128), F32),
+        pltpu.VMEM((40, 128), F32),
         pltpu.SemaphoreType.DMA((span_i // GROUP,)),
         pltpu.SemaphoreType.DMA((COPIES,)),
         pltpu.SemaphoreType.DMA((COPIES,)),

time: 52.7 us -> 52.7 us (level)
  no operation moved by 1% of the time
where the time goes in v2:
time: 52.7 us; the launch traced here: 52.6 us
  Pallas kernels  50 us (95%)
  local copies, waits for them, and re-layouts  1.18 us (2%)
  other arithmetic  0.71 us (1%)
  between operations  0.64 us (1%)
    pallas_call x1, Pallas kernels, local(): pl.pallas_call(kernel, out_shape=jax.ShapeDtypeStruct((16, 128), F32), in...  50 us
    slice x2, local copies, waits for them, and re-layouts, local(): return (out[:4, :RANK], out[8:14, :RANK], out[4:8, :RANK])  1.18 us

profile of v2, /device:TPU:1, one launch (start us, length us, event | category | flops | bytes accessed | tf_op | source)
XLA Modules:
  0.0 52.6 jit_solution(8373415707690920898)
XLA Ops:
  0.6 0.7 %select_maximum_fusion.start_ref = f32[16,64]{1,0:T(8,128)S(1)} fusion(f32[4,64]{1,0:T(4,128)} %param.5, f32[6,64]{1,0:T(8,128)} %param.4), kind=kLoop, calls=%fused_computation | loop fusion | flops 5120 | bytes 6656 | tf_op jit(solution)/shard_map/concatenate | solution.py:437
  1.3 50.0 %shard_map.58 = f32[16,128]{1,0:T(8,128)S(1)} custom-call(f32[32,384,128]{2,1,0:T(8,128)} %t_ref.1, f32[16,64]{1,0:T(8,128)S(1)} %select_maximum_fusion.start_ref), custom_call_target="tpu_custom_call" | custom-call | tf_op jit(solution)/shard_map/pallas_call | solution.py:440
  51.4 0.6 %fusion = (f32[4,64]{1,0:T(4,128)}, f32[4,64]{1,0:T(4,128)}) fusion(f32[16,128]{1,0:T(8,128)S(1)} %shard_map.58), kind=kLoop, calls=%fused_computation.3 | loop fusion | bytes 4096 | tf_op jit(solution)/shard_map/slice | solution.py:450
  52.0 0.6 %slice.10 = f32[6,64]{1,0:T(8,128)} slice(f32[16,128]{1,0:T(8,128)S(1)} %shard_map.58), slice={[8:14], [0:64]} | slice | bytes 3072 | tf_op jit(solution)/shard_map/slice | solution.py:450
